TPU v7x, 32 devices: a whole 2x2x4 slice. The times are simulated.
32 devices in a mesh: ctx: 8 (over z, y), head: 4 (over x, core).
Axes of the slice: x: 2, y: 2, z: 4, core: 2. Of those that a mesh axis runs over, the one named last changes fastest.
Arguments:
- queries: bfloat16 [2048, 6144], P(('ctx', 'head')), may hold values from -120 to 120
- keys: bfloat16 [2048, 1024], P(('ctx', 'head')), may hold values from -6 to 6
- values: bfloat16 [2048, 1024], P(('ctx', 'head')), may hold values from -6 to 6
- outputs: bfloat16 [2048, 6144], P(('ctx', 'head')), may hold values from -6 to 6
- out_grad: bfloat16 [2048, 6144], P(('ctx', 'head')), may hold values from -6 to 6
- frame_lists: int32 [8, 5], P('ctx'), may hold values from -1 to 7, as said below
Outputs:
- grad_queries: bfloat16 [2048, 6144], P('ctx', 'head')
- key_gradient: bfloat16 [2048, 1024], P('ctx', 'head')
- value_gradient: bfloat16 [2048, 1024], P('ctx', 'head')
Inputs may be any that keep to these rules, and one draw needn't show every extreme that they name: `frame_lists`: entry o of the list of query frame f is f - o or -1 (always -1 where f - o < 0); entry 0 is f; entry 4 is f - 4 for every frame f divisible by 3 with f >= 4.
All inputs are finite; a program needn't handle non-finite values.
Results may differ from a plain program's by a relative error of at most 0.005.
Values may be sent and summed in bfloat16 or wider, within the bound.
A program may use at most 64 MiB of HBM per device.

v0:
```python
import functools

import jax
import jax.numpy as jnp
from jax import lax
from jax.experimental import pallas as pl
from jax.experimental.pallas import tpu as pltpu
from jax.sharding import PartitionSpec as P

MESH = pl.DeviceIdType.MESH
HEAD_SIZE = 128
FRAME = 256
REACH = 4
BLOCKS = REACH + 1
LOG2E = 1.4426950408889634
LAST = (((1,), (1,)), ((), ()))


def dot(a, b):
    return jnp.dot(a, b, preferred_element_type=jnp.float32)


def dot_last(a, b):
    return lax.dot_general(a, b, LAST, preferred_element_type=jnp.float32)


def kernel(
    n_ctx, n_head, kv_count, width,
    q_ref, k_ref, v_ref, o_ref, g_ref, list_ref,
    dq_ref, dk_ref, dv_ref,
    qb, gb, kvb, g_loc, o_loc, lists, d_out, d_in, delta, sc, share, dq_sum, acc, out_buf, in_buf,
    own_sem, in_sem, a_send, a_recv, d_send, d_recv, f_send, f_recv, r_send, r_recv,
):
    c = lax.axis_index("ctx")
    h = lax.axis_index("head")
    y = lax.rem(c, 2)
    across = c + 1 - 2 * y
    rows = q_ref.shape[0]
    tokens = rows * n_head
    heads = kv_count * width
    scale = HEAD_SIZE ** -0.5

    g_in = pltpu.make_async_copy(g_ref, g_loc, in_sem.at[0])
    o_in = pltpu.make_async_copy(o_ref, o_loc, in_sem.at[1])
    l_in = pltpu.make_async_copy(list_ref, lists, in_sem.at[2])
    g_in.start()
    o_in.start()
    l_in.start()

    barrier = pltpu.get_barrier_semaphore()
    peers = [lax.rem(h + r, n_head) for r in range(1, n_head)]
    for p in peers:
        pl.semaphore_signal(barrier, inc=1, device_id=(c, p), device_id_type=MESH)
    pl.semaphore_signal(barrier, inc=1, device_id=(across, h), device_id_type=MESH)

    @pl.when(c + 2 < n_ctx)
    def _():
        pl.semaphore_signal(barrier, inc=1, device_id=(c + 2, h), device_id_type=MESH)

    @pl.when(c >= 2)
    def _():
        pl.semaphore_signal(barrier, inc=1, device_id=(c - 2, h), device_id_type=MESH)

    ends = jnp.where(c + 2 < n_ctx, 1, 0) + jnp.where(c >= 2, 1, 0)
    pl.semaphore_wait(barrier, n_head + ends)

    my_rows = pl.ds(pl.multiple_of(h * rows, rows), rows)

    def piece(what, j, p):
        if what < 2:
            start = pl.multiple_of((p * kv_count + j) * HEAD_SIZE, HEAD_SIZE)
            ref = (k_ref, v_ref)[what]
            return ref.at[:, pl.ds(start, HEAD_SIZE)], kvb.at[j, 0, what, my_rows, :]
        span = width * HEAD_SIZE
        start = pl.multiple_of((p * kv_count + j) * span, HEAD_SIZE)
        ref, place = ((q_ref, qb), (g_ref, gb))[what - 2]
        return ref.at[:, pl.ds(start, span)], place.at[j, my_rows, :]

    def remote(what, j, r):
        source, place = piece(what, j, peers[r])
        return pltpu.make_async_remote_copy(
            src_ref=source, dst_ref=place, send_sem=a_send.at[r, j, what], recv_sem=a_recv.at[r, j, what],
            device_id=(c, peers[r]), device_id_type=MESH,
        )

    def local(what, j):
        source, place = piece(what, j, h)
        return pltpu.make_async_copy(source, place, own_sem.at[j, what])

    def regroup(whats, j, do):
        for what in whats:
            for r in range(n_head - 1):
                do(remote(what, j, r))
            do(local(what, j))

    def start(copy):
        copy.start()

    def wait(copy):
        copy.wait()

    def forward(j, what, k):
        source, slot, target, holds = (
            (0, 2, c + 2, c + 2 < n_ctx),
            (2 * y, 1, across, c >= 2 * y),
            (2, 4, c + 2, (c + 2 < n_ctx) & (c >= 2)),
            (2 + 2 * y, 3, across, c >= 2 + 2 * y),
        )[k]
        copy = pltpu.make_async_remote_copy(
            src_ref=kvb.at[j, source, what], dst_ref=kvb.at[j, slot, what], send_sem=f_send.at[j, what, k],
            recv_sem=f_recv.at[j, what, k], device_id=(target, h), device_id_type=MESH,
        )
        return copy, holds

    def forward_start(j, what, k):
        copy, holds = forward(j, what, k)

        @pl.when(holds)
        def _():
            copy.start()

    def forward_sent(j, what, k):
        copy, holds = forward(j, what, k)

        @pl.when(holds)
        def _():
            copy.wait_send()

    def forward_here(j, what, k):
        copy, _ = forward(j, what, k)

        @pl.when(c >= (2, 1, 4, 3)[k])
        def _():
            copy.wait_recv()

    def spread(j, what, stage):
        if stage == 0:
            forward_start(j, what, 0)

            @pl.when(y == 0)
            def _():
                forward(j, what, 1)[0].start()
        elif stage == 1:
            forward_here(j, what, 0)
            forward_start(j, what, 2)

            @pl.when((y == 1) & (c >= 2))
            def _():
                forward(j, what, 1)[0].start()

            @pl.when((y == 0) & (c >= 2))
            def _():
                forward(j, what, 3)[0].start()
        elif stage == 2:
            forward_here(j, what, 2)

            @pl.when((y == 1) & (c >= 4))
            def _():
                forward(j, what, 3)[0].start()
        else:
            forward_here(j, what, 1)
            forward_here(j, what, 3)
            for k in range(4):
                forward_sent(j, what, k)

    def back(j, k):
        source, target, holds, comes = (
            (0, across, c >= 1, across >= 1),
            (1, across, c >= 3, across >= 3),
            (2, c - 2, c >= 4, (c >= 2) & (c + 2 < n_ctx)),
            (3, c - 2, c >= 2, c + 2 < n_ctx),
        )[k]
        copy = pltpu.make_async_remote_copy(
            src_ref=out_buf.at[j, source], dst_ref=in_buf.at[j, k], send_sem=r_send.at[j, k],
            recv_sem=r_recv.at[j, k], device_id=(target, h), device_id_type=MESH,
        )
        return copy, holds, comes

    def back_start(j, k, slot):
        copy, holds, _ = back(j, k)

        @pl.when(holds)
        def _():
            out_buf[j, k] = acc[j, slot].astype(jnp.bfloat16)
            copy.start()

    def back_add(j, k, slot):
        copy, _, comes = back(j, k)

        @pl.when(comes)
        def _():
            copy.wait_recv()
            acc[j, slot] += in_buf[j, k].astype(jnp.float32)

    def back_after(j, t):
        if t == 0:
            back_start(j, 1, 3)
        elif t == 1:
            back_start(j, 0, 1)
        elif t == 2:
            @pl.when(y == 0)
            def _():
                back_start(j, 2, 4)
        elif t == 3:
            @pl.when(y == 1)
            def _():
                back_add(j, 1, 4)
                back_start(j, 2, 4)

    def back_late(j):
        @pl.when(y == 0)
        def _():
            back_add(j, 1, 2)
        back_add(j, 0, 2 * y)
        back_add(j, 2, 2)
        back_start(j, 3, 2)

    def back_end(j):
        back_add(j, 3, 0)
        cols = slice(j * HEAD_SIZE, (j + 1) * HEAD_SIZE)
        dk_ref[:, cols] = (acc[j, 0, 0] * scale).astype(jnp.bfloat16)
        dv_ref[:, cols] = acc[j, 0, 1].astype(jnp.bfloat16)
        for k in range(4):
            copy, holds, _ = back(j, k)

            @pl.when(holds)
            def _():
                copy.wait_send()

    for what in (0, 2, 1, 3):
        regroup((what,), 0, start)

    for o in range(1, BLOCKS):
        @pl.when(c < o)
        def _():
            kvb[:, o] = jnp.zeros((kv_count, 2, tokens, HEAD_SIZE), jnp.bfloat16)
    regroup((0,), 0, wait)
    spread(0, 0, 0)

    d_out[...] = jnp.zeros(d_out.shape, jnp.float32)
    g_in.wait()
    o_in.wait()
    l_in.wait()
    ones = jnp.ones((16, HEAD_SIZE), jnp.bfloat16)

    def delta_of(p, carry):
        for i in range(heads):
            cols = pl.ds(pl.multiple_of((p * heads + i) * HEAD_SIZE, HEAD_SIZE), HEAD_SIZE)
            product = g_loc[:, cols].astype(jnp.float32) * o_loc[:, cols].astype(jnp.float32)
            high = product.astype(jnp.bfloat16)
            low = (product - high.astype(jnp.float32)).astype(jnp.bfloat16)
            sums = dot_last(ones, high) + dot_last(ones, low)
            d_out[p, i:i + 1, 0:rows] = sums[0:1]
        return carry

    lax.fori_loop(0, n_head, delta_of, 0)

    def delta_copy(r):
        return pltpu.make_async_remote_copy(
            src_ref=d_out.at[peers[r]], dst_ref=d_in.at[h], send_sem=d_send.at[r], recv_sem=d_recv.at[r],
            device_id=(c, peers[r]), device_id_type=MESH,
        )

    for r in range(n_head - 1):
        delta_copy(r).start()
    d_in[h] = d_out[h]

    spread(0, 0, 1)
    if kv_count > 1:
        regroup((0, 2), 1, start)
    spread(0, 0, 2)
    spread(0, 0, 3)
    for r in range(n_head - 1):
        delta_copy(r).wait()
    for i in range(n_head):
        delta[:, i * rows:(i + 1) * rows] = d_in[i, :, 0:rows]

    bars = []
    for o in range(BLOCKS):
        listed = lists[0, 0] == c - o
        for e in range(1, lists.shape[1]):
            listed = listed | (lists[0, e] == c - o)
        bars.append(jnp.where(listed & (c - o >= 0), 0.0, jnp.inf).astype(jnp.float32))

    def span(w):
        return pl.ds(pl.multiple_of(w * HEAD_SIZE, HEAD_SIZE), HEAD_SIZE)

    def exponentials(j, w):
        q = qb[j, :, span(w)]
        peak = None
        for o in range(BLOCKS):
            s = dot_last(kvb[j, o, 0], q) * (scale * LOG2E)
            sc[w, o] = s
            top = jnp.max(s, axis=0, keepdims=True) - bars[o]
            peak = top if peak is None else jnp.maximum(peak, top)
        total = jnp.zeros_like(peak)
        for o in range(BLOCKS):
            e = jnp.exp2(sc[w, o] - (peak + bars[o]))
            sc[w, o] = e
            total += jnp.sum(e, axis=0, keepdims=True)
        share[pl.ds(w, 1), :] = 1.0 / total
        dq_sum[w] = jnp.zeros(dq_sum.shape[1:], jnp.float32)

    def gradients(j, o):
        value = kvb[j, o, 1]
        key_t = kvb[j, o, 0].T
        dk = dv = None
        for w in range(width):
            cols = slice(w * HEAD_SIZE, (w + 1) * HEAD_SIZE)
            q = qb[j, :, cols]
            g = gb[j, :, cols]
            row = delta[j * width + w:j * width + w + 1, :]
            p = sc[w, o] * share[w:w + 1, :]
            ds = (p * (dot_last(value, g) - row)).astype(jnp.bfloat16)
            dv_term = dot(p.astype(jnp.bfloat16), g)
            dk_term = dot(ds, q)
            dq_sum[w] += dot(key_t, ds)
            dv = dv_term if dv is None else dv + dv_term
            dk = dk_term if dk is None else dk + dk_term
        acc[j, o, 0] = dk
        acc[j, o, 1] = dv

    third = width // 3

    for j in range(kv_count):
        more = j + 1 < kv_count
        regroup((2,), j, wait)
        regroup((1,), j, wait)
        spread(j, 1, 0)

        def first(w, carry):
            for at in (1, 2):
                @pl.when(w == at * third)
                def _():
                    spread(j, 1, at)
                    if j > 0:
                        (back_late, back_end)[at - 1](j - 1)
            exponentials(j, w)
            return carry

        lax.fori_loop(0, width, first, 0)
        spread(j, 1, 3)
        regroup((3,), j, wait)
        if more:
            regroup((1, 3), j + 1, start)
            regroup((0,), j + 1, wait)
            spread(j + 1, 0, 0)

        def second(t, carry):
            gradients(j, lax.rem(3 + 3 * t, BLOCKS))
            for at in range(4):
                @pl.when(t == at)
                def _():
                    back_after(j, at)
                    if more and 1 <= at <= 2:
                        spread(j + 1, 0, at)
            return carry

        lax.fori_loop(0, BLOCKS, second, 0)
        if more:
            spread(j + 1, 0, 3)
        else:
            back_late(j)
        for w in range(width):
            i = j * width + w
            dq_ref[:, i * HEAD_SIZE:(i + 1) * HEAD_SIZE] = (dq_sum[w] * scale).T.astype(jnp.bfloat16)
        if j + 2 < kv_count:
            regroup((0, 2), j + 2, start)
    back_end(kv_count - 1)


def hand_over(*refs):
    sems = refs[-1]
    count = (len(refs) - 1) // 2
    copies = [pltpu.make_async_copy(refs[i], refs[count + i], sems.at[i]) for i in range(count)]
    for copy in copies:
        copy.start()
    for copy in copies:
        copy.wait()


def on_device(n_ctx, n_head, queries, keys, values, outputs, out_grad, frame_lists):
    rows = queries.shape[0]
    tokens = rows * n_head
    kv_count = keys.shape[1] // HEAD_SIZE // n_head
    heads = queries.shape[1] // HEAD_SIZE // n_head
    width = heads // kv_count
    padded = -(-heads // 16) * 16
    assert tokens == FRAME and n_ctx % 2 == 0
    bf, f32 = jnp.bfloat16, jnp.float32
    any_spec = pl.BlockSpec(memory_space=pl.ANY)
    vmem = pl.BlockSpec(memory_space=pltpu.VMEM)
    dma = pltpu.SemaphoreType.DMA
    results = pl.pallas_call(
        functools.partial(kernel, n_ctx, n_head, kv_count, width),
        out_shape=(
            jax.ShapeDtypeStruct((tokens, heads * HEAD_SIZE), bf),
            jax.ShapeDtypeStruct((tokens, kv_count * HEAD_SIZE), bf),
            jax.ShapeDtypeStruct((tokens, kv_count * HEAD_SIZE), bf),
        ),
        in_specs=[any_spec] * 6,
        out_specs=(vmem, vmem, vmem),
        scratch_shapes=[
            pltpu.VMEM((kv_count, tokens, width * HEAD_SIZE), bf),
            pltpu.VMEM((kv_count, tokens, width * HEAD_SIZE), bf),
            pltpu.VMEM((kv_count, BLOCKS, 2, tokens, HEAD_SIZE), bf),
            pltpu.VMEM(out_grad.shape, bf),
            pltpu.VMEM(outputs.shape, bf),
            pltpu.SMEM(frame_lists.shape, jnp.int32),
            pltpu.VMEM((n_head, padded, HEAD_SIZE), f32),
            pltpu.VMEM((n_head, padded, HEAD_SIZE), f32),
            pltpu.VMEM((padded, tokens), f32),
            pltpu.VMEM((width, BLOCKS, tokens, tokens), f32),
            pltpu.VMEM((-(-width // 8) * 8, tokens), f32),
            pltpu.VMEM((width, HEAD_SIZE, tokens), f32),
            pltpu.VMEM((kv_count, BLOCKS, 2, tokens, HEAD_SIZE), f32),
            pltpu.VMEM((kv_count, 4, 2, tokens, HEAD_SIZE), bf),
            pltpu.VMEM((kv_count, 4, 2, tokens, HEAD_SIZE), bf),
            dma((kv_count, 4)),
            dma((3,)),
            dma((n_head - 1, kv_count, 4)),
            dma((n_head - 1, kv_count, 4)),
            dma((n_head - 1,)),
            dma((n_head - 1,)),
            dma((kv_count, 2, 4)),
            dma((kv_count, 2, 4)),
            dma((kv_count, 4)),
            dma((kv_count, 4)),
        ],
        compiler_params=pltpu.CompilerParams(
            collective_id=0, has_side_effects=True, vmem_limit_bytes=60 * 1024 * 1024
        ),
    )(queries, keys, values, outputs, out_grad, frame_lists)
    return pl.pallas_call(
        hand_over,
        out_shape=[jax.ShapeDtypeStruct(x.shape, x.dtype) for x in results],
        in_specs=[any_spec] * 3,
        out_specs=[vmem] * 3,
        scratch_shapes=[dma((3,))],
    )(*results)


def solution(mesh):
    split = P(("ctx", "head"), None)
    return jax.shard_map(
        functools.partial(on_device, mesh.shape["ctx"], mesh.shape["head"]),
        mesh=mesh,
        in_specs=(split,) * 5 + (P("ctx", None),),
        out_specs=(P("ctx", "head"),) * 3,
        check_vma=False,
    )
```

profile of v0, /device:TPU:0, one launch (start us, length us, event | category | flops | bytes accessed | tf_op | source)
XLA Modules:
  0.0 62.8 jit_solution(10777757653526270138)
XLA Ops:
  0.6 60.0 %shard_map.85 = (bf16[256,1536]{1,0:T(8,128)(2,1)}, bf16[256,256]{1,0:T(8,128)(2,1)}, bf16[256,256]{1,0:T(8,128)(2,1)}) custom-call(bf16[64,6144]{1,0:T(8,128)(2,1)} %q_ref.1, bf16[64,1024]{1,0:T(8,128)(2,1)} %k_ref.1, bf16[64,1024]{1,0:T(8,128)(2,1)} %v_ref.1, bf16[64,6144]{1,0:T(8,128)(2,1)} %o_ref.1, bf16[64,6144]{1,0:T(8,128)(2,1)} %g_ref.1, s32[1,5]{1,0:T(1,128)} %list_ref.1), custom_call_target="tpu_custom_call" | custom-call | tf_op jit(solution)/shard_map/pallas_call | solution.py:394
  60.7 2.2 %shard_map.86 = (bf16[256,1536]{1,0:T(8,128)(2,1)}, bf16[256,256]{1,0:T(8,128)(2,1)}, bf16[256,256]{1,0:T(8,128)(2,1)}) custom-call(bf16[256,1536]{1,0:T(8,128)(2,1)} %get-tuple-element.6.refs_0_, bf16[256,256]{1,0:T(8,128)(2,1)} %get-tuple-element.7.refs_1_, bf16[256,256]{1,0:T(8,128)(2,1)} %get-tuple-element.8.refs_2_), custom_call_target="tpu_custom_call" | custom-call | tf_op jit(solution)/shard_map/pallas_call | solution.py:434
where the time goes:
time: 63 us; the launch traced here: 62.8 us
  Pallas kernels  62.2 us (99%)
  between operations  0.64 us (1%)
    pallas_call x1, Pallas kernels, on_device(): pl.pallas_call(functools.partial(kernel, n_ctx, n_head, kv_count, width),...  60 us
    pallas_call x1, Pallas kernels, on_device(): pl.pallas_call(hand_over, out_shape=[jax.ShapeDtypeStruct(x.shape, x.dtyp...  2.16 us

commit v1 on v0

--- a/solution.py
+++ b/solution.py
@@ -28,7 +28,7 @@
     n_ctx, n_head, kv_count, width,
     q_ref, k_ref, v_ref, o_ref, g_ref, list_ref,
     dq_ref, dk_ref, dv_ref,
-    qb, gb, kvb, g_loc, o_loc, lists, d_out, d_in, delta, sc, share, dq_sum, acc, out_buf, in_buf,
+    qb, gb, kvb, q_loc, g_loc, o_loc, lists, d_out, d_in, delta, sc, share, dq_sum, acc, out_buf, in_buf,
     own_sem, in_sem, a_send, a_recv, d_send, d_recv, f_send, f_recv, r_send, r_recv,
 ):
     c = lax.axis_index("ctx")
@@ -43,6 +43,8 @@
     g_in = pltpu.make_async_copy(g_ref, g_loc, in_sem.at[0])
     o_in = pltpu.make_async_copy(o_ref, o_loc, in_sem.at[1])
     l_in = pltpu.make_async_copy(list_ref, lists, in_sem.at[2])
+    q_in = pltpu.make_async_copy(q_ref, q_loc, in_sem.at[3])
+    q_in.start()
     g_in.start()
     o_in.start()
     l_in.start()
@@ -73,7 +75,7 @@
             return ref.at[:, pl.ds(start, HEAD_SIZE)], kvb.at[j, 0, what, my_rows, :]
         span = width * HEAD_SIZE
         start = pl.multiple_of((p * kv_count + j) * span, HEAD_SIZE)
-        ref, place = ((q_ref, qb), (g_ref, gb))[what - 2]
+        ref, place = ((q_loc, qb), (g_loc, gb))[what - 2]
         return ref.at[:, pl.ds(start, span)], place.at[j, my_rows, :]
 
     def remote(what, j, r):
@@ -227,8 +229,11 @@
             def _():
                 copy.wait_send()
 
-    for what in (0, 2, 1, 3):
-        regroup((what,), 0, start)
+    regroup((0,), 0, start)
+    q_in.wait()
+    regroup((2, 1), 0, start)
+    g_in.wait()
+    regroup((3,), 0, start)
 
     for o in range(1, BLOCKS):
         @pl.when(c < o)
@@ -238,7 +243,6 @@
     spread(0, 0, 0)
 
     d_out[...] = jnp.zeros(d_out.shape, jnp.float32)
-    g_in.wait()
     o_in.wait()
     l_in.wait()
     ones = jnp.ones((16, HEAD_SIZE), jnp.bfloat16)
@@ -404,6 +408,7 @@
             pltpu.VMEM((kv_count, tokens, width * HEAD_SIZE), bf),
             pltpu.VMEM((kv_count, tokens, width * HEAD_SIZE), bf),
             pltpu.VMEM((kv_count, BLOCKS, 2, tokens, HEAD_SIZE), bf),
+            pltpu.VMEM(queries.shape, bf),
             pltpu.VMEM(out_grad.shape, bf),
             pltpu.VMEM(outputs.shape, bf),
             pltpu.SMEM(frame_lists.shape, jnp.int32),
@@ -417,7 +422,7 @@
             pltpu.VMEM((kv_count, 4, 2, tokens, HEAD_SIZE), bf),
             pltpu.VMEM((kv_count, 4, 2, tokens, HEAD_SIZE), bf),
             dma((kv_count, 4)),
-            dma((3,)),
+            dma((4,)),
             dma((n_head - 1, kv_count, 4)),
             dma((n_head - 1, kv_count, 4)),
             dma((n_head - 1,)),

time: 63 us -> 63 us (level)
  no operation moved by 1% of the time
where the time goes in v1:
time: 63 us; the launch traced here: 62.8 us
  Pallas kernels  62.2 us (99%)
  between operations  0.64 us (1%)
    pallas_call x1, Pallas kernels, on_device(): pl.pallas_call(functools.partial(kernel, n_ctx, n_head, kv_count, width),...  60 us
    pallas_call x1, Pallas kernels, on_device(): pl.pallas_call(hand_over, out_shape=[jax.ShapeDtypeStruct(x.shape, x.dtyp...  2.16 us

profile of v1, /device:TPU:0, one launch (start us, length us, event | category | flops | bytes accessed | tf_op | source)
XLA Modules:
  0.0 62.8 jit_solution(14291336908751545697)
XLA Ops:
  0.6 60.0 %shard_map.85 = (bf16[256,1536]{1,0:T(8,128)(2,1)}, bf16[256,256]{1,0:T(8,128)(2,1)}, bf16[256,256]{1,0:T(8,128)(2,1)}) custom-call(bf16[64,6144]{1,0:T(8,128)(2,1)} %q_ref.1, bf16[64,1024]{1,0:T(8,128)(2,1)} %k_ref.1, bf16[64,1024]{1,0:T(8,128)(2,1)} %v_ref.1, bf16[64,6144]{1,0:T(8,128)(2,1)} %o_ref.1, bf16[64,6144]{1,0:T(8,128)(2,1)} %g_ref.1, s32[1,5]{1,0:T(1,128)} %list_ref.1), custom_call_target="tpu_custom_call" | custom-call | tf_op jit(solution)/shard_map/pallas_call | solution.py:398
  60.7 2.2 %shard_map.86 = (bf16[256,1536]{1,0:T(8,128)(2,1)}, bf16[256,256]{1,0:T(8,128)(2,1)}, bf16[256,256]{1,0:T(8,128)(2,1)}) custom-call(bf16[256,1536]{1,0:T(8,128)(2,1)} %get-tuple-element.6.refs_0_, bf16[256,256]{1,0:T(8,128)(2,1)} %get-tuple-element.7.refs_1_, bf16[256,256]{1,0:T(8,128)(2,1)} %get-tuple-element.8.refs_2_), custom_call_target="tpu_custom_call" | custom-call | tf_op jit(solution)/shard_map/pallas_call | solution.py:439
